TPU v7x, 32 devices: a whole 2x2x4 slice. The times are simulated.
32 devices in a mesh: basin: 2 (over y), tm: 16 (over z, x, core).
Axes of the slice: x: 2, y: 2, z: 4, core: 2. Of those that a mesh axis runs over, the one named last changes fastest.
Arguments:
- perturbation: bfloat16 [64, 512, 512], P(('basin', 'tm')), parts along dimension 0, may hold values from -0.02734375 to 0.02734375
- hours_live: int32 [32], P(('basin', 'tm')), parts along dimension 0, may hold values from 1 to 2, as said below
- start_hour: int32 [1], replicated, may hold values from 0 to 15
- release_coeffs: bfloat16 [1024, 2048], P('basin'), parts along dimension 0, may hold values from -6 to 6
- batch_of_column: int32 [4096], P('basin'), parts along dimension 0, may hold values from 0 to 63
- batch_amplitude: float32 [128], P('basin'), parts along dimension 0, may hold values from 0.1 to 3
Outputs:
- panels: bfloat16 [32, 512, 2048], P(('basin', 'tm')), parts along dimension 0
There are 2 independent parts, one for each index of `basin`. A program takes and returns all parts, laid end to end along the dimension named above; an argument that names none is the same for every part. Nothing has to cross between parts.
Inputs may be any that keep to these rules, and one draw needn't show every extreme that they name: `hours_live`: some owner has all 2 hours live.
All inputs are finite; a program needn't handle non-finite values.
Results may differ from a plain program's by a relative error of at most 0.0057.
Values sent between devices are 32-bit elements; how exact they have to be, the bound alone decides.
A program may use at most 64 MiB of HBM per device.

v0:
```python
import jax
import jax.numpy as jnp
from jax import lax
from jax.sharding import PartitionSpec as P


def passed_along(value, axis, steps):
    count = lax.axis_size(axis)
    first, last = (max(0, -steps), min(count, count - steps))
    return lax.ppermute(value, axis, [(source, source + steps) for source in range(first, last)])


def later_times_earlier(earlier, later):
    return jnp.dot(
        later, earlier, precision=lax.Precision.HIGHEST, preferred_element_type=jnp.float32
    )


def on_device(
    perturbation, hours_live, start_hour, release_coeffs, batch_of_column, batch_amplitude
):
    hours_dev = perturbation.shape[0]
    order = perturbation.shape[1]
    owner = lax.axis_index("tm")
    start = start_hour[0]
    eye = jnp.eye(order, dtype=jnp.float32)
    local = eye
    for j in range(hours_dev):
        hour = owner * hours_dev + j
        alive = jnp.logical_and(j < hours_live[0], hour >= start)
        operator = eye + jnp.where(alive, perturbation[j].astype(jnp.float32), jnp.float32(0.0))
        local = later_times_earlier(local, operator)
    match = (
        batch_of_column[:, None] == jnp.arange(batch_amplitude.shape[0], dtype=jnp.int32)[None, :]
    )
    column_scale = jnp.sum(jnp.where(match, batch_amplitude[None, :], jnp.float32(0.0)), axis=1)
    release = (release_coeffs.astype(jnp.float32) * column_scale[None, :]).astype(jnp.bfloat16)
    levels = (lax.axis_size("tm") - 1).bit_length()
    reach = local
    for level in range(levels):
        distance = 1 << level
        earlier = passed_along(reach, "tm", distance)
        reach = jnp.where(owner >= distance, later_times_earlier(earlier, reach), reach)
    panel = jnp.dot(reach.astype(jnp.bfloat16), release, preferred_element_type=jnp.float32)
    return panel.astype(jnp.bfloat16)[None, :, :]


def solution(mesh):
    in_specs = (
        P(("basin", "tm"), None, None),
        P(("basin", "tm")),
        P(),
        P("basin", None),
        P("basin"),
        P("basin"),
    )
    out_specs = P(("basin", "tm"), None, None)
    return jax.shard_map(
        on_device, mesh=mesh, in_specs=in_specs, out_specs=out_specs, check_vma=False
    )
```

profile of v0, /device:TPU:25, one launch (start us, length us, event | category | flops | bytes accessed | tf_op | source)
XLA Modules:
  0.0 129.6 jit_solution(2455554023314886091)
XLA Ops:
  0.0 0.0 copy-start
  1.4 2.0 %fusion.3 = f32[512,512]{1,0:T(8,128)S(1)} fusion(bf16[2,512,512]{2,1,0:T(8,128)(2,1)} %param.6, pred[]{:T(512)S(6)} %and.8), kind=kOutput, calls=%fused_computation.11 | convolution fusion | flops 1612185600 | bytes 1572865 | tf_op jit(solution)/shard_map/dot_general | solution.py:14
  3.5 0.0 copy-done
  3.5 1.9 %fusion.4 = f32[512,512]{1,0:T(8,128)S(1)} fusion(f32[512,512]{1,0:T(8,128)S(1)} %fusion.3, bf16[2,512,512]{2,1,0:T(8,128)(2,1)S(1)} %copy-done, pred[]{:T(512)S(6)} %and.7), kind=kOutput, calls=%fused_computation.12 | convolution fusion | flops 1611923456 | bytes 2621441 | tf_op jit(solution)/shard_map/dot_general | solution.py:14
  5.4 3.7 %collective-permute-start = (f32[512,512]{1,0:T(8,128)S(1)}, f32[512,512]{1,0:T(8,128)S(1)}, u32[]{:S(2)}, u32[]{:S(2)}) collective-permute-start(f32[512,512]{1,0:T(8,128)S(1)} %fusion.4), channel_id=1, source_target_pairs={{0,1},{1,2},{2,3},{3,4},{4,5},{5,6},{6,7},{7,8},{8,9},{9,10},{10,1... | collective-permute-start | bytes 3145736 | tf_op jit(solution)/shard_map/ppermute | solution.py:10
  9.1 11.7 %collective-permute-done = f32[512,512]{1,0:T(8,128)S(1)} collective-permute-done((f32[512,512]{1,0:T(8,128)S(1)}, f32[512,512]{1,0:T(8,128)S(1)}, u32[]{:S(2)}, u32[]{:S(2)}) %collective-permute-start) | collective-permute-done | bytes 1048608 | tf_op jit(solution)/shard_map/ppermute | solution.py:10
  20.8 1.8 %convolution_select_fusion.3 = f32[512,512]{1,0:T(8,128)S(1)} fusion(f32[512,512]{1,0:T(8,128)S(1)} %fusion.4, f32[512,512]{1,0:T(8,128)S(1)} %collective-permute-done, pred[]{:T(512)S(6)} %ge.21), kind=kOutput, calls=%fused_computation.7 | convolution fusion | flops 1610874880 | bytes 3145729 | tf_op jit(solution)/shard_map/dot_general | solution.py:14
  22.6 1.9 %collective-permute-start.1 = (f32[512,512]{1,0:T(8,128)S(1)}, f32[512,512]{1,0:T(8,128)S(1)}, u32[]{:S(2)}, u32[]{:S(2)}) collective-permute-start(f32[512,512]{1,0:T(8,128)S(1)} %convolution_select_fusion.3), channel_id=1, source_target_pairs={{0,2},{1,3},{2,4},{3,5},{4,6},{5,7},{6,8},{7,9},{8,10},{9,11},{10,... | collective-permute-start | bytes 3145736 | tf_op jit(solution)/shard_map/ppermute | solution.py:10
  24.6 23.2 %collective-permute-done.1 = f32[512,512]{1,0:T(8,128)S(1)} collective-permute-done((f32[512,512]{1,0:T(8,128)S(1)}, f32[512,512]{1,0:T(8,128)S(1)}, u32[]{:S(2)}, u32[]{:S(2)}) %collective-permute-start.1) | collective-permute-done | bytes 1048608 | tf_op jit(solution)/shard_map/ppermute | solution.py:10
  47.8 1.8 %convolution_select_fusion.2 = f32[512,512]{1,0:T(8,128)S(1)} fusion(f32[512,512]{1,0:T(8,128)S(1)} %convolution_select_fusion.3, f32[512,512]{1,0:T(8,128)S(1)} %collective-permute-done.1, pred[]{:T(512)S(6)} %ge.20), kind=kOutput, calls=%fused_computation.6 | convolution fusion | flops 1610874880 | bytes 3145729 | tf_op jit(solution)/shard_map/dot_general | solution.py:14
  49.6 0.0 copy-start.1
  49.7 0.0 copy-start.2
  49.7 1.3 collective-permute-start.2
  51.0 22.0 %collective-permute-done.2 = f32[512,512]{1,0:T(8,128)S(1)} collective-permute-done((f32[512,512]{1,0:T(8,128)S(1)}, f32[512,512]{1,0:T(8,128)S(1)}, u32[]{:S(2)}, u32[]{:S(2)}) %collective-permute-start.2) | collective-permute-done | bytes 1048608 | tf_op jit(solution)/shard_map/ppermute | solution.py:10
  73.0 1.8 %convolution_select_fusion.1 = f32[512,512]{1,0:T(8,128)S(1)} fusion(f32[512,512]{1,0:T(8,128)S(1)} %convolution_select_fusion.2, f32[512,512]{1,0:T(8,128)S(1)} %collective-permute-done.2, pred[]{:T(512)S(6)} %ge.19), kind=kOutput, calls=%fused_computation.5 | convolution fusion | flops 1610874880 | bytes 3145729 | tf_op jit(solution)/shard_map/dot_general | solution.py:14
  74.9 1.3 collective-permute-start.3
  76.2 0.0 copy-done.1
  76.2 0.0 copy-done.2
  76.2 0.0 copy-start.3
  76.2 0.2 select_reduce_fusion
  76.4 48.7 %collective-permute-done.3 = f32[512,512]{1,0:T(8,128)S(1)} collective-permute-done((f32[512,512]{1,0:T(8,128)S(1)}, f32[512,512]{1,0:T(8,128)S(1)}, u32[]{:S(2)}, u32[]{:S(2)}) %collective-permute-start.3) | collective-permute-done | bytes 1048608 | tf_op jit(solution)/shard_map/ppermute | solution.py:10
  125.1 1.8 %fusion.2 = bf16[512,512]{1,0:T(8,128)(2,1)S(1)} fusion(f32[512,512]{1,0:T(8,128)S(1)} %convolution_select_fusion.1, f32[512,512]{1,0:T(8,128)S(1)} %collective-permute-done.3, pred[]{:T(512)S(6)} %ge.18), kind=kOutput, calls=%fused_computation.10 | convolution fusion | flops 1611137024 | bytes 2621441 | tf_op jit(solution)/shard_map/dot_general | solution.py:14
  127.0 0.0 copy-done.3
  127.0 2.6 %fusion = bf16[1,512,2048]{2,1,0:T(8,128)(2,1)} fusion(bf16[512,512]{1,0:T(8,128)(2,1)S(1)} %fusion.2, bf16[512,2048]{1,0:T(8,128)(2,1)S(1)} %copy-done.3, f32[2048]{0:T(1024)S(1)} %select_reduce_fusion), kind=kOutput, calls=%fused_computation.2 | convolution fusion | flops 1077936128 | bytes 4726784 | tf_op jit(solution)/shard_map/dot_general | solution.py:44
Async XLA Ops:
  0.0 3.5 %copy-start = (bf16[2,512,512]{2,1,0:T(8,128)(2,1)S(1)}, bf16[2,512,512]{2,1,0:T(8,128)(2,1)}, u32[]{:S(2)}) copy-start(bf16[2,512,512]{2,1,0:T(8,128)(2,1)} %param.6) | copy-start | bytes 3145732
  5.4 15.4 %collective-permute-start = (f32[512,512]{1,0:T(8,128)S(1)}, f32[512,512]{1,0:T(8,128)S(1)}, u32[]{:S(2)}, u32[]{:S(2)}) collective-permute-start(f32[512,512]{1,0:T(8,128)S(1)} %fusion.4), channel_id=1, source_target_pairs={{0,1},{1,2},{2,3},{3,4},{4,5},{5,6},{6,7},{7,8},{8,9},{9,10},{10,1... | collective-permute-start | bytes 3145736 | tf_op jit(solution)/shard_map/ppermute | solution.py:10
  22.6 25.2 %collective-permute-start.1 = (f32[512,512]{1,0:T(8,128)S(1)}, f32[512,512]{1,0:T(8,128)S(1)}, u32[]{:S(2)}, u32[]{:S(2)}) collective-permute-start(f32[512,512]{1,0:T(8,128)S(1)} %convolution_select_fusion.3), channel_id=1, source_target_pairs={{0,2},{1,3},{2,4},{3,5},{4,6},{5,7},{6,8},{7,9},{8,10},{9,11},{10,... | collective-permute-start | bytes 3145736 | tf_op jit(solution)/shard_map/ppermute | solution.py:10
  49.6 26.5 %copy-start.1 = (s32[2048]{0:T(1024)S(1)}, s32[2048]{0:T(1024)}, u32[]{:S(2)}) copy-start(s32[2048]{0:T(1024)} %param.10) | copy-start | bytes 24580
  49.7 26.5 %copy-start.2 = (f32[64]{0:T(128)S(1)}, f32[64]{0:T(128)}, u32[]{:S(2)}) copy-start(f32[64]{0:T(128)} %param.11) | copy-start | bytes 772
  49.7 23.3 %collective-permute-start.2 = (f32[512,512]{1,0:T(8,128)S(1)}, f32[512,512]{1,0:T(8,128)S(1)}, u32[]{:S(2)}, u32[]{:S(2)}) collective-permute-start(f32[512,512]{1,0:T(8,128)S(1)} %convolution_select_fusion.2), channel_id=1, source_target_pairs={{0,4},{1,5},{2,6},{3,7},{4,8},{5,9},{6,10},{7,11},{8,12},{9,13},{1... | collective-permute-start | bytes 3145736 | tf_op jit(solution)/shard_map/ppermute | solution.py:10
  74.9 50.2 %collective-permute-start.3 = (f32[512,512]{1,0:T(8,128)S(1)}, f32[512,512]{1,0:T(8,128)S(1)}, u32[]{:S(2)}, u32[]{:S(2)}) collective-permute-start(f32[512,512]{1,0:T(8,128)S(1)} %convolution_select_fusion.1), channel_id=1, source_target_pairs={{0,8},{1,9},{2,10},{3,11},{4,12},{5,13},{6,14},{7,15},{16,24},{17,... | collective-permute-start | bytes 3145736 | tf_op jit(solution)/shard_map/ppermute | solution.py:10
  76.2 50.8 %copy-start.3 = (bf16[512,2048]{1,0:T(8,128)(2,1)S(1)}, bf16[512,2048]{1,0:T(8,128)(2,1)}, u32[]{:S(2)}) copy-start(bf16[512,2048]{1,0:T(8,128)(2,1)} %param.9) | copy-start | bytes 6291460
where the time goes:
time: 130 us
  waiting for transfers between devices  106 us (82%)
  matrix products  13.9 us (11%)
  starting transfers between devices  8.18 us (6%)
  between operations  1.56 us (1%)
    ppermute x4, waiting for transfers between devices, passed_along(): lax.ppermute(value, axis, [(source, source + steps) for source in range(f...  106 us
    dot_general x6, matrix products, later_times_earlier(): jnp.dot(later, earlier, precision=lax.Precision.HIGHEST, preferred_elemen...  11.3 us
    ppermute x4, starting transfers between devices, passed_along(): lax.ppermute(value, axis, [(source, source + steps) for source in range(f...  8.18 us
  transfers between devices with their start and end apart: 4, of which 4 were waited for; matrix products, arithmetic and copies ran while one was open for 0% of the time, Pallas kernels for 0%

commit v1 on v0

v1 whole, which is shorter than its diff:
```python
import functools
import jax
import jax.numpy as jnp
from jax import lax
from jax.experimental import pallas as pl
from jax.experimental.pallas import tpu as pltpu
from jax.sharding import PartitionSpec as P

MESH = pl.DeviceIdType.MESH
QUAD = 4
X_CHUNKS = 4
CHAIN_CHUNKS = 4


def halves(value):
    high = value.astype(jnp.bfloat16)
    return high, (value - high.astype(jnp.float32)).astype(jnp.bfloat16)


def mul(a, b):
    return jnp.dot(a, b, preferred_element_type=jnp.float32)


def times(left, right, right_high, right_low):
    high, low = halves(left)
    return left + right + (mul(high, right_high) + (mul(high, right_low) + mul(low, right_high)))


def kernel(
    count,
    hours_live,
    start_hour,
    pert,
    coeffs,
    batch,
    amplitude,
    panel,
    local2,
    chip2,
    quad,
    reach_in,
    within,
    sent,
    right_high,
    right_low,
    quad_high,
    quad_low,
    release,
    reach_out,
    core_sem,
    x_sem,
    xf_sem,
    z_sem,
    ef_sem,
    ex_sem,
    exf_sem,
):
    order = pert.shape[1]
    me = lax.axis_index("tm")
    core = me % 2
    x = (me // 2) % 2
    lane = me % QUAD
    q = me // QUAD
    quads = count // QUAD
    core_mate = me + 1 - 2 * core
    x_mate = me + 2 - 4 * x
    has_next = q < quads - 1
    has_prev = q > 0

    barrier = pltpu.get_barrier_semaphore()
    for mate in (core_mate, x_mate):
        pl.semaphore_signal(barrier, inc=1, device_id={"tm": mate}, device_id_type=MESH)

    @pl.when(has_next)
    def _():
        pl.semaphore_signal(barrier, inc=1, device_id={"tm": me + QUAD}, device_id_type=MESH)

    @pl.when(has_prev)
    def _():
        pl.semaphore_signal(barrier, inc=1, device_id={"tm": me - QUAD}, device_id_type=MESH)

    scales = []
    for j in range(pert.shape[0]):
        alive = jnp.logical_and(j < hours_live[0], me * pert.shape[0] + j >= start_hour[0])
        scales.append(jnp.where(alive, jnp.float32(1.0), jnp.float32(0.0)))
    total = pert[0].astype(jnp.float32) * scales[0]
    for j in range(1, pert.shape[0]):
        left = pert[j].astype(jnp.float32) * scales[j]
        high, low = halves(total)
        factor = left.astype(jnp.bfloat16)
        product = mul(factor, high)
        if j > 1:
            product = product + mul(factor, low)
        total = total + left + product
    local2[core] = total.T

    pl.semaphore_wait(barrier, 2 + has_next.astype(jnp.int32) + has_prev.astype(jnp.int32))

    def remote(src, dst, send, recv, device):
        return pltpu.make_async_remote_copy(
            src_ref=src,
            dst_ref=dst,
            send_sem=send,
            recv_sem=recv,
            device_id={"tm": device},
            device_id_type=MESH,
        )

    to_core = remote(
        local2.at[core], local2.at[core], core_sem.at[0], core_sem.at[1], core_mate
    )
    to_core.start()
    to_core.wait()

    high, low = halves(local2[1])
    right_high[...] = high
    right_low[...] = low
    half = order // 2
    step = half // X_CHUNKS

    def x_rows(c, s):
        return pl.ds(pl.multiple_of(c * half + s * step, step), step)

    def chip_rows(rows):
        chip2[x, rows] = times(local2[0, rows], local2[1, rows], right_high[...], right_low[...])

    def x_copy(s):
        rows = x_rows(core, s)
        return remote(
            chip2.at[x, rows], chip2.at[x, rows], x_sem.at[0, s], x_sem.at[1, s], x_mate
        )

    def x_forward(s):
        rows = x_rows(core, s)
        return remote(
            chip2.at[1 - x, rows],
            chip2.at[1 - x, rows],
            xf_sem.at[0, s],
            xf_sem.at[1, s],
            core_mate,
        )

    for s in range(X_CHUNKS):
        chip_rows(x_rows(core, s))
        x_copy(s).start()
    chip_rows(pl.ds(pl.multiple_of((1 - core) * half, half), half))

    ids = lax.broadcasted_iota(jnp.int32, (amplitude.shape[0], batch.shape[1]), 0)
    column_scale = jnp.sum(
        jnp.where(ids == batch[...], amplitude[...], jnp.float32(0.0)), axis=0, keepdims=True
    )
    release[...] = (coeffs[...].astype(jnp.float32) * column_scale).astype(jnp.bfloat16)

    for s in range(X_CHUNKS):
        x_copy(s).wait_recv()
        x_forward(s).start()
    for s in range(X_CHUNKS):
        x_forward(s).wait_recv()

    high, low = halves(chip2[1])
    right_high[...] = high
    right_low[...] = low
    quad[...] = times(chip2[0], chip2[1], right_high[...], right_low[...])
    high, low = halves(quad[...])
    quad_high[...] = high
    quad_low[...] = low

    share = order // QUAD
    part = share // CHAIN_CHUNKS

    def lane_rows(which, s):
        return pl.ds(pl.multiple_of(which * share + s * part, part), part)

    def chain(s):
        return remote(
            sent.at[pl.ds(s * part, part)],
            reach_in.at[lane_rows(lane, s)],
            z_sem.at[0, s],
            z_sem.at[1, s],
            me + QUAD,
        )

    def to_mate(sem, which, device, s):
        rows = lane_rows(which, s)
        return remote(reach_in.at[rows], reach_in.at[rows], sem.at[0, s], sem.at[1, s], device)

    own_core = functools.partial(to_mate, ef_sem, lane, core_mate)
    own_x = functools.partial(to_mate, ex_sem, lane, x_mate)
    x_lane = lane + 2 - 4 * x
    other_core = functools.partial(to_mate, exf_sem, x_lane, core_mate)

    @pl.when(q == 0)
    def _():
        reach_in[...] = jnp.zeros_like(reach_in)

    def chain_step(s):
        rows = lane_rows(lane, s)

        @pl.when(has_prev)
        def _():
            chain(s).wait_recv()
            own_x(s).start()
            own_core(s).start()

        @pl.when(has_next)
        def _():
            sent[s * part : (s + 1) * part] = times(
                reach_in[rows], quad[rows], quad_high[...], quad_low[...]
            )
            chain(s).start()

    def share_step(s):
        @pl.when(has_prev)
        def _():
            to_mate(ex_sem, x_lane, x_mate, s).wait_recv()
            other_core(s).start()

    for s in range(CHAIN_CHUNKS):
        chain_step(s)
        if s:
            share_step(s - 1)

    @pl.when(lane == 0)
    def _():
        within[...] = local2[0]

    @pl.when(lane == 1)
    def _():
        within[...] = chip2[0]

    @pl.when(lane == 2)
    def _():
        high, low = halves(local2[0])
        within[...] = times(chip2[0], local2[0], high, low)

    @pl.when(lane == 3)
    def _():
        within[...] = quad[...]

    high, low = halves(within[...])
    right_high[...] = high
    right_low[...] = low
    share_step(CHAIN_CHUNKS - 1)

    @pl.when(has_prev)
    def _():
        for s in range(CHAIN_CHUNKS):
            to_mate(ef_sem, lane + 1 - 2 * core, core_mate, s).wait_recv()
            to_mate(exf_sem, x_lane + 1 - 2 * core, core_mate, s).wait_recv()

    diagonal = lax.broadcasted_iota(jnp.int32, (order, order), 0) == lax.broadcasted_iota(
        jnp.int32, (order, order), 1
    )
    reach = times(reach_in[...], within[...], right_high[...], right_low[...])
    reach = reach + jnp.where(diagonal, jnp.float32(1.0), jnp.float32(0.0))
    reach_out[...] = reach.T.astype(jnp.bfloat16)
    width = panel.shape[2] // 4
    for s in range(4):
        columns = slice(s * width, (s + 1) * width)
        panel[0, :, columns] = mul(reach_out[...], release[:, columns]).astype(jnp.bfloat16)

    for s in range(X_CHUNKS):
        x_copy(s).wait_send()
        x_forward(s).wait_send()
    for s in range(CHAIN_CHUNKS):

        @pl.when(has_next)
        def _():
            chain(s).wait_send()

        @pl.when(has_prev)
        def _():
            own_x(s).wait_send()
            own_core(s).wait_send()
            other_core(s).wait_send()


def on_device(
    count, perturbation, hours_live, start_hour, release_coeffs, batch_of_column, batch_amplitude
):
    order = perturbation.shape[1]
    columns = release_coeffs.shape[1]
    vmem = pl.BlockSpec(memory_space=pltpu.VMEM)
    smem = pl.BlockSpec(memory_space=pltpu.SMEM)
    f32, bf16 = jnp.float32, jnp.bfloat16
    square = (order, order)
    return pl.pallas_call(
        functools.partial(kernel, count),
        out_shape=jax.ShapeDtypeStruct((1, order, columns), bf16),
        in_specs=[smem, smem, vmem, vmem, vmem, vmem],
        out_specs=vmem,
        scratch_shapes=[
            pltpu.VMEM((2,) + square, f32),
            pltpu.VMEM((2,) + square, f32),
            pltpu.VMEM(square, f32),
            pltpu.VMEM(square, f32),
            pltpu.VMEM(square, f32),
            pltpu.VMEM((order // QUAD, order), f32),
            pltpu.VMEM(square, bf16),
            pltpu.VMEM(square, bf16),
            pltpu.VMEM(square, bf16),
            pltpu.VMEM(square, bf16),
            pltpu.VMEM((order, columns), bf16),
            pltpu.VMEM(square, bf16),
            pltpu.SemaphoreType.DMA((2,)),
            pltpu.SemaphoreType.DMA((2, X_CHUNKS)),
            pltpu.SemaphoreType.DMA((2, X_CHUNKS)),
            pltpu.SemaphoreType.DMA((2, CHAIN_CHUNKS)),
            pltpu.SemaphoreType.DMA((2, CHAIN_CHUNKS)),
            pltpu.SemaphoreType.DMA((2, CHAIN_CHUNKS)),
            pltpu.SemaphoreType.DMA((2, CHAIN_CHUNKS)),
        ],
        compiler_params=pltpu.CompilerParams(
            collective_id=0, has_side_effects=True, vmem_limit_bytes=48 * 1024 * 1024
        ),
    )(
        hours_live,
        start_hour,
        perturbation,
        release_coeffs,
        batch_of_column[None, :],
        batch_amplitude[:, None],
    )


def solution(mesh):
    in_specs = (
        P(("basin", "tm"), None, None),
        P(("basin", "tm")),
        P(),
        P("basin", None),
        P("basin"),
        P("basin"),
    )
    out_specs = P(("basin", "tm"), None, None)
    return jax.shard_map(
        functools.partial(on_device, mesh.shape["tm"]),
        mesh=mesh,
        in_specs=in_specs,
        out_specs=out_specs,
        check_vma=False,
    )
```

time: 130 us -> 49.9 us (0.38)
  waiting for transfers between devices: 106 us -> 0 us
  Pallas kernels: 0 us -> 42.8 us
  matrix products: 13.9 us -> 0 us
  starting transfers between devices: 8.18 us -> 0 us
  local copies, waits for them, and re-layouts: 0.02 us -> 5.58 us
    ppermute x4 -> x0, waiting for transfers between devices: 106 us -> none  [passed_along(): lax.ppermute(value, axis, [(source, source + steps) for source in range(f...]
    pallas_call x0 -> x1, Pallas kernels: none -> 42.8 us  [on_device(): pl.pallas_call(functools.partial(kernel, count), out_shape=jax.ShapeDtype...]
    dot_general x7 -> x0, matrix products: 13.9 us -> none  [the longest x6 11.3 us: later_times_earlier(): jnp.dot(later, earlier, precision=lax.Precision.HIGHEST, preferred_elemen...]
    ppermute x4 -> x0, starting transfers between devices: 8.18 us -> none  [passed_along(): lax.ppermute(value, axis, [(source, source + steps) for source in range(f...]
    unnamed x8 -> x7, local copies, waits for them, and re-layouts: 0.02 us -> 4.83 us
  transfers between devices with their start and end apart: 4 -> 0, of which waited for: 4 -> 0; matrix products, arithmetic and copies ran while one was open for 0% -> 0% of each run, Pallas kernels for 0% -> 0%
where the time goes in v1:
time: 49.9 us; the launch traced here: 49.7 us
  Pallas kernels  42.8 us (86%)
  local copies, waits for them, and re-layouts  5.58 us (11%)
  between operations  1.31 us (3%)
    pallas_call x1, Pallas kernels, on_device(): pl.pallas_call(functools.partial(kernel, count), out_shape=jax.ShapeDtype...  42.8 us
    unnamed x7, local copies, waits for them, and re-layouts  4.83 us

profile of v1, /device:TPU:25, one launch (start us, length us, event | category | flops | bytes accessed | tf_op | source)
XLA Modules:
  0.0 49.7 jit_solution(7157437512487751425)
XLA Ops:
  1.3 0.7 %copy.7.amplitude = f32[64,1]{1,0:T(8,128)S(1)} copy(f32[64,1]{0,1:T(1,128)} %bitcast.3) | data formatting | bytes 512 | tf_op jit(solution)/shard_map/broadcast_in_dim | solution.py:322
  2.0 0.0 copy-start
  2.0 1.6 %copy-done = bf16[512,2048]{1,0:T(8,128)(2,1)S(1)} copy-done((bf16[512,2048]{1,0:T(8,128)(2,1)S(1)}, bf16[512,2048]{1,0:T(8,128)(2,1)}, u32[]{:S(2)}) %copy-start) | copy-done | bytes 2097176
  3.6 0.0 copy-start.1
  3.6 1.2 %copy-done.1 = bf16[2,512,512]{2,1,0:T(8,128)(2,1)S(1)} copy-done((bf16[2,512,512]{2,1,0:T(8,128)(2,1)S(1)}, bf16[2,512,512]{2,1,0:T(8,128)(2,1)}, u32[]{:S(2)}) %copy-start.1) | copy-done | bytes 1048600
  4.9 0.0 copy-start.2
  4.9 0.7 %copy-done.2 = s32[2048]{0:T(1024)S(1)} copy-done((s32[2048]{0:T(1024)S(1)}, s32[2048]{0:T(1024)}, u32[]{:S(2)}) %copy-start.2) | copy-done | bytes 8216
  5.6 42.8 %shard_map.64 = bf16[1,512,2048]{2,1,0:T(8,128)(2,1)S(1)} custom-call(s32[1]{0:T(128)S(6)} %copy.9.hours_live, s32[1]{0:T(128)S(6)} %copy.10.start_hour, bf16[2,512,512]{2,1,0:T(8,128)(2,1)S(1)} %copy-done.1, bf16[512,2048]{1,0:T(8,128)(2,1)S(1)} %copy-done, s32[1,2048]{1,0:T(1,128)S(1)} %bitcast.2, f32[64,1]{1,0:T(8,128)S(1)} %copy.7.amplitude), custom_call_target="tpu_custom_call" | custom-call | tf_op jit(solution)/shard_map/pallas_call | solution.py:287
  48.4 1.3 %copy.11 = bf16[1,512,2048]{2,1,0:T(8,128)(2,1)} copy(bf16[1,512,2048]{2,1,0:T(8,128)(2,1)S(1)} %shard_map.64) | data formatting | bytes 4194304
Async XLA Ops:
  2.0 1.6 %copy-start = (bf16[512,2048]{1,0:T(8,128)(2,1)S(1)}, bf16[512,2048]{1,0:T(8,128)(2,1)}, u32[]{:S(2)}) copy-start(bf16[512,2048]{1,0:T(8,128)(2,1)} %coeffs.1) | copy-start | bytes 6291460
  3.6 1.2 %copy-start.1 = (bf16[2,512,512]{2,1,0:T(8,128)(2,1)S(1)}, bf16[2,512,512]{2,1,0:T(8,128)(2,1)}, u32[]{:S(2)}) copy-start(bf16[2,512,512]{2,1,0:T(8,128)(2,1)} %pert.1) | copy-start | bytes 3145732
  4.9 0.7 %copy-start.2 = (s32[2048]{0:T(1024)S(1)}, s32[2048]{0:T(1024)}, u32[]{:S(2)}) copy-start(s32[2048]{0:T(1024)} %param.10) | copy-start | bytes 24580

commit v2 on v0

v2 whole, which is shorter than its diff:
```python
import functools
import jax
import jax.numpy as jnp
from jax import lax
from jax.experimental import pallas as pl
from jax.experimental.pallas import tpu as pltpu
from jax.sharding import PartitionSpec as P

MESH = pl.DeviceIdType.MESH
QUAD = 4
UNITS = 32


def halves(value):
    high = value.astype(jnp.bfloat16)
    return high, (value - high.astype(jnp.float32)).astype(jnp.bfloat16)


def mul(a, b):
    return jnp.dot(a, b, preferred_element_type=jnp.float32)


def times(left, right, right_high, right_low):
    high, low = halves(left)
    return left + right + (mul(high, right_high) + (mul(high, right_low) + mul(low, right_high)))


def kernel(
    count,
    hours_live,
    start_hour,
    amplitude,
    pert_in,
    coeffs_in,
    batch_in,
    reach_out,
    release,
    pert,
    coeffs,
    batch,
    local2,
    chip2,
    quad,
    reach_in,
    within,
    sent,
    back,
    right_high,
    right_low,
    quad_high,
    quad_low,
    in_sem,
    core_sem,
    x_sem,
    xf_sem,
    back_sem,
    z_sem,
    ef_sem,
    ex_sem,
    exf_sem,
):
    order = pert.shape[1]
    unit = order // UNITS
    per_core = UNITS // 2
    per_lane = UNITS // QUAD
    me = lax.axis_index("tm")
    core = me % 2
    x = (me // 2) % 2
    lane = me % QUAD
    q = me // QUAD
    core_mate = me + 1 - 2 * core
    x_mate = me + 2 - 4 * x
    has_next = q < count // QUAD - 1
    has_prev = q > 0
    first = q == 0
    gets_x = jnp.logical_or(has_prev, x == 1)
    sends_x = jnp.logical_or(has_prev, x == 0)

    fetches = [
        pltpu.make_async_copy(src, dst, in_sem.at[i])
        for i, (src, dst) in enumerate(((pert_in, pert), (coeffs_in, coeffs), (batch_in, batch)))
    ]
    for fetch in fetches:
        fetch.start()
    barrier = pltpu.get_barrier_semaphore()
    for mate in (core_mate, x_mate):
        pl.semaphore_signal(barrier, inc=1, device_id={"tm": mate}, device_id_type=MESH)

    @pl.when(has_next)
    def _():
        pl.semaphore_signal(barrier, inc=1, device_id={"tm": me + QUAD}, device_id_type=MESH)

    @pl.when(has_prev)
    def _():
        pl.semaphore_signal(barrier, inc=1, device_id={"tm": me - QUAD}, device_id_type=MESH)

    scales = []
    for j in range(pert.shape[0]):
        alive = jnp.logical_and(j < hours_live[0], me * pert.shape[0] + j >= start_hour[0])
        scales.append(jnp.where(alive, jnp.float32(1.0), jnp.float32(0.0)))
    fetches[0].wait()
    total = pert[0].astype(jnp.float32) * scales[0]
    for j in range(1, pert.shape[0]):
        left = pert[j].astype(jnp.float32) * scales[j]
        high, low = halves(total)
        factor = left.astype(jnp.bfloat16)
        product = mul(factor, high)
        if j > 1:
            product = product + mul(factor, low)
        total = total + left + product
    local2[core] = total.T

    pl.semaphore_wait(barrier, 2 + has_next.astype(jnp.int32) + has_prev.astype(jnp.int32))

    def remote(src, dst, sems, i, device):
        return pltpu.make_async_remote_copy(
            src_ref=src,
            dst_ref=dst,
            send_sem=sems.at[0, i],
            recv_sem=sems.at[1, i],
            device_id={"tm": device},
            device_id_type=MESH,
        )

    def same(ref, sems, i, device):
        return remote(ref, ref, sems, i, device)

    def rows_at(chunk):
        return pl.ds(pl.multiple_of(chunk * unit, unit), unit)

    group = order // QUAD

    def to_core(owner, g):
        return same(local2.at[owner, pl.ds(g * group, group)], core_sem, g, core_mate)

    for g in range(QUAD):
        to_core(core, g).start()

    @pl.when(core == 0)
    def _():
        for g in range(QUAD):
            to_core(1 - core, g).wait_recv()

    high, low = halves(local2[1])
    right_high[...] = high
    right_low[...] = low

    def x_copy(side, c, j):
        return same(chip2.at[side, rows_at(2 * j + c)], x_sem, j, x_mate)

    def x_forward(c, j):
        return same(chip2.at[1 - x, rows_at(2 * j + c)], xf_sem, j, core_mate)

    for g in range(QUAD):

        @pl.when(core == 1)
        def _():
            to_core(1 - core, g).wait_recv()

        rows = slice(g * group, (g + 1) * group)
        chip2[x, rows] = times(local2[0, rows], local2[1, rows], right_high[...], right_low[...])

        @pl.when(sends_x)
        def _():
            for j in range(g * per_core // QUAD, (g + 1) * per_core // QUAD):
                x_copy(x, core, j).start()

    def make_release():
        fetches[1].wait()
        fetches[2].wait()
        ids = batch[...]
        column_scale = jnp.zeros(ids.shape, jnp.float32)
        for b in range(amplitude.shape[0]):
            column_scale = jnp.where(ids == b, amplitude[b], column_scale)
        release[...] = (coeffs[...].astype(jnp.float32) * column_scale).astype(jnp.bfloat16)

    pl.when(has_prev)(make_release)

    def send_back(s):
        here = pl.ds(pl.multiple_of(s * unit, unit), unit)
        return remote(back.at[here], sent.at[here], back_sem, s, x_mate)

    def chain(c_lane, s):
        here = pl.ds(pl.multiple_of(s * unit, unit), unit)
        chunk = (c_lane // 2) * per_core + 2 * s + c_lane % 2
        return remote(sent.at[here], reach_in.at[rows_at(chunk)], z_sem, s, me + QUAD)

    @pl.when(jnp.logical_and(first, x == 1))
    def _():
        high, low = halves(chip2[1])
        right_high[...] = high
        right_low[...] = low

        def step(j):
            x_copy(1 - x, core, j).wait_recv()
            x_forward(core, j).start()
            rows = rows_at(2 * j + core)
            return times(chip2[0, rows], chip2[1, rows], right_high[...], right_low[...])

        @pl.loop(0, per_lane)
        def _(j):
            back[pl.ds(pl.multiple_of(j * unit, unit), unit)] = step(j)
            send_back(j).start()

        @pl.loop(0, per_lane)
        def _(s):
            sent[pl.ds(pl.multiple_of(s * unit, unit), unit)] = step(s + per_lane)

            @pl.when(has_next)
            def _():
                chain(lane, s).start()

    @pl.when(jnp.logical_and(first, x == 0))
    def _():
        @pl.loop(0, per_lane)
        def _(s):
            send_back(s).wait_recv()

            @pl.when(has_next)
            def _():
                chain(lane, s).start()

    @pl.when(has_prev)
    def _():
        @pl.loop(0, per_core)
        def _(j):
            x_copy(1 - x, core, j).wait_recv()
            x_forward(core, j).start()

    pl.when(first)(make_release)

    @pl.when(gets_x)
    def _():
        @pl.loop(0, per_core)
        def _(j):
            x_forward(1 - core, j).wait_recv()

        high, low = halves(chip2[1])
        right_high[...] = high
        right_low[...] = low
        quad[...] = times(chip2[0], chip2[1], right_high[...], right_low[...])
        high, low = halves(quad[...])
        quad_high[...] = high
        quad_low[...] = low

    def make_within():
        @pl.when(lane == 0)
        def _():
            within[...] = local2[0]

        @pl.when(lane == 1)
        def _():
            within[...] = chip2[0]

        @pl.when(lane == 2)
        def _():
            high, low = halves(local2[0])
            within[...] = times(chip2[0], local2[0], high, low)

        @pl.when(lane == 3)
        def _():
            within[...] = quad[...]

        high, low = halves(within[...])
        right_high[...] = high
        right_low[...] = low

    pl.when(jnp.logical_not(has_next))(make_within)

    def lane_rows(c_lane, s):
        return rows_at((c_lane // 2) * per_core + 2 * s + c_lane % 2)

    def shared(sems, c_lane, device, s):
        return same(reach_in.at[lane_rows(c_lane, s)], sems, s, device)

    x_lane = lane + 2 - 4 * x
    core_lane = lane + 1 - 2 * core
    xc_lane = x_lane + 1 - 2 * core

    def share_x(s):
        shared(ex_sem, x_lane, x_mate, s).wait_recv()
        shared(exf_sem, x_lane, core_mate, s).start()

    @pl.when(has_prev)
    def _():
        @pl.loop(0, per_lane)
        def _(s):
            chain(lane, s).wait_recv()
            shared(ex_sem, lane, x_mate, s).start()
            shared(ef_sem, lane, core_mate, s).start()

            @pl.when(has_next)
            def _():
                rows = lane_rows(lane, s)
                sent[pl.ds(pl.multiple_of(s * unit, unit), unit)] = times(
                    reach_in[rows], quad[rows], quad_high[...], quad_low[...]
                )
                chain(lane, s).start()

            @pl.when(s > 1)
            def _():
                share_x(s - 2)

    pl.when(has_next)(make_within)

    def finish(value, start, size):
        shape = (size, order)
        diagonal = start + lax.broadcasted_iota(
            jnp.int32, shape, 0
        ) == lax.broadcasted_iota(jnp.int32, shape, 1)
        value = value + jnp.where(diagonal, jnp.float32(1.0), jnp.float32(0.0))
        reach_out[:, pl.ds(start, size)] = value.T.astype(jnp.bfloat16)

    @pl.when(first)
    def _():
        finish(within[...], 0, order)

    half = order // 2

    def finish_half(side):
        start = pl.multiple_of(side * half, half)
        rows = pl.ds(start, half)
        finish(
            times(reach_in[rows], within[rows], right_high[...], right_low[...]), start, half
        )

    @pl.when(has_prev)
    def _():
        share_x(per_lane - 2)
        share_x(per_lane - 1)

        @pl.loop(0, per_lane)
        def _(s):
            shared(ef_sem, core_lane, core_mate, s).wait_recv()

        finish_half(x)

        @pl.loop(0, per_lane)
        def _(s):
            shared(exf_sem, xc_lane, core_mate, s).wait_recv()

        finish_half(1 - x)

    for g in range(QUAD):
        to_core(core, g).wait_send()

    @pl.when(sends_x)
    def _():
        @pl.loop(0, per_core)
        def _(j):
            x_copy(x, core, j).wait_send()

    @pl.when(gets_x)
    def _():
        @pl.loop(0, per_core)
        def _(j):
            x_forward(core, j).wait_send()

    @pl.when(jnp.logical_and(first, x == 1))
    def _():
        @pl.loop(0, per_lane)
        def _(s):
            send_back(s).wait_send()

    @pl.when(has_next)
    def _():
        @pl.loop(0, per_lane)
        def _(s):
            chain(lane, s).wait_send()

    @pl.when(has_prev)
    def _():
        @pl.loop(0, per_lane)
        def _(s):
            shared(ex_sem, lane, x_mate, s).wait_send()
            shared(ef_sem, lane, core_mate, s).wait_send()
            shared(exf_sem, x_lane, core_mate, s).wait_send()


def on_device(
    count, perturbation, hours_live, start_hour, release_coeffs, batch_of_column, batch_amplitude
):
    order = perturbation.shape[1]
    columns = release_coeffs.shape[1]
    vmem = pl.BlockSpec(memory_space=pltpu.VMEM)
    smem = pl.BlockSpec(memory_space=pltpu.SMEM)
    anywhere = pl.BlockSpec(memory_space=pl.ANY)
    f32, bf16 = jnp.float32, jnp.bfloat16
    square = (order, order)
    sems = lambda n: pltpu.SemaphoreType.DMA((2, n))
    reach, release = pl.pallas_call(
        functools.partial(kernel, count),
        out_shape=(
            jax.ShapeDtypeStruct(square, bf16),
            jax.ShapeDtypeStruct((order, columns), bf16),
        ),
        in_specs=[smem, smem, smem, anywhere, anywhere, anywhere],
        out_specs=(vmem, vmem),
        scratch_shapes=[
            pltpu.VMEM(perturbation.shape, bf16),
            pltpu.VMEM((order, columns), bf16),
            pltpu.VMEM((1, columns), jnp.int32),
            pltpu.VMEM((2,) + square, f32),
            pltpu.VMEM((2,) + square, f32),
            pltpu.VMEM(square, f32),
            pltpu.VMEM(square, f32),
            pltpu.VMEM(square, f32),
            pltpu.VMEM((order // QUAD, order), f32),
            pltpu.VMEM((order // QUAD, order), f32),
            pltpu.VMEM(square, bf16),
            pltpu.VMEM(square, bf16),
            pltpu.VMEM(square, bf16),
            pltpu.VMEM(square, bf16),
            pltpu.SemaphoreType.DMA((3,)),
            sems(QUAD),
            sems(UNITS // 2),
            sems(UNITS // 2),
            sems(UNITS // QUAD),
            sems(UNITS // QUAD),
            sems(UNITS // QUAD),
            sems(UNITS // QUAD),
            sems(UNITS // QUAD),
        ],
        compiler_params=pltpu.CompilerParams(
            collective_id=0, has_side_effects=True, vmem_limit_bytes=48 * 1024 * 1024
        ),
    )(
        hours_live,
        start_hour,
        batch_amplitude,
        perturbation,
        release_coeffs,
        batch_of_column[None, :],
    )
    panel = jnp.dot(reach, release, preferred_element_type=jnp.float32)
    return panel.astype(bf16)[None, :, :]


def solution(mesh):
    in_specs = (
        P(("basin", "tm"), None, None),
        P(("basin", "tm")),
        P(),
        P("basin", None),
        P("basin"),
        P("basin"),
    )
    out_specs = P(("basin", "tm"), None, None)
    return jax.shard_map(
        functools.partial(on_device, mesh.shape["tm"]),
        mesh=mesh,
        in_specs=in_specs,
        out_specs=out_specs,
        check_vma=False,
    )
```

time: 130 us -> 45.8 us (0.35)
  waiting for transfers between devices: 106 us -> 0 us
  Pallas kernels: 0 us -> 37.5 us
  matrix products: 13.9 us -> 2.58 us
  starting transfers between devices: 8.18 us -> 0 us
  local copies, waits for them, and re-layouts: 0.02 us -> 4.16 us
    ppermute x4 -> x0, waiting for transfers between devices: 106 us -> none  [passed_along(): lax.ppermute(value, axis, [(source, source + steps) for source in range(f...]
    pallas_call x0 -> x1, Pallas kernels: none -> 37.5 us  [on_device(): pl.pallas_call(functools.partial(kernel, count), out_shape=(jax.ShapeDtyp...]
    dot_general x7 -> x1, matrix products: 13.9 us -> 2.58 us  [on_device(): panel = jnp.dot(reach, release, preferred_element_type=jnp.float32)]
    ppermute x4 -> x0, starting transfers between devices: 8.18 us -> none  [passed_along(): lax.ppermute(value, axis, [(source, source + steps) for source in range(f...]
    unnamed x8, local copies, waits for them, and re-layouts: 0.02 us -> 4.16 us
  transfers between devices with their start and end apart: 4 -> 0, of which waited for: 4 -> 0; matrix products, arithmetic and copies ran while one was open for 0% -> 0% of each run, Pallas kernels for 0% -> 0%
where the time goes in v2:
time: 45.8 us; the launch traced here: 45.5 us
  Pallas kernels  37.5 us (82%)
  local copies, waits for them, and re-layouts  4.16 us (9%)
  matrix products  2.58 us (6%)
  between operations  1.32 us (3%)
    pallas_call x1, Pallas kernels, on_device(): pl.pallas_call(functools.partial(kernel, count), out_shape=(jax.ShapeDtyp...  37.5 us
    unnamed x8, local copies, waits for them, and re-layouts  4.16 us
    dot_general x1, matrix products, on_device(): panel = jnp.dot(reach, release, preferred_element_type=jnp.float32)  2.58 us

profile of v2, /device:TPU:25, one launch (start us, length us, event | category | flops | bytes accessed | tf_op | source)
XLA Modules:
  0.0 45.5 jit_solution(18172190472818914623)
XLA Ops:
  1.3 0.0 copy-start
  1.3 1.6 %copy-done = bf16[512,2048]{1,0:T(8,128)(2,1)S(1)} copy-done((bf16[512,2048]{1,0:T(8,128)(2,1)S(1)}, bf16[512,2048]{1,0:T(8,128)(2,1)}, u32[]{:S(2)}) %copy-start) | copy-done | bytes 2097176
  2.9 0.0 copy-start.1
  2.9 1.2 %copy-done.1 = bf16[2,512,512]{2,1,0:T(8,128)(2,1)S(1)} copy-done((bf16[2,512,512]{2,1,0:T(8,128)(2,1)S(1)}, bf16[2,512,512]{2,1,0:T(8,128)(2,1)}, u32[]{:S(2)}) %copy-start.1) | copy-done | bytes 1048600
  4.1 0.0 copy-start.2
  4.1 0.7 %copy-done.2 = s32[2048]{0:T(1024)S(1)} copy-done((s32[2048]{0:T(1024)S(1)}, s32[2048]{0:T(1024)}, u32[]{:S(2)}) %copy-start.2) | copy-done | bytes 8216
  4.8 0.0 copy-start.3
  4.8 0.7 %copy-done.3 = f32[64]{0:T(128)S(1)} copy-done((f32[64]{0:T(128)S(1)}, f32[64]{0:T(128)}, u32[]{:S(2)}) %copy-start.3) | copy-done | bytes 280
  5.5 37.5 %shard_map.64 = (bf16[512,512]{1,0:T(8,128)(2,1)S(1)}, bf16[512,2048]{1,0:T(8,128)(2,1)S(1)}) custom-call(s32[1]{0:T(128)S(6)} %copy.7.hours_live, s32[1]{0:T(128)S(6)} %copy.8.start_hour, f32[64]{0:T(128)S(1)} %copy-done.3, bf16[2,512,512]{2,1,0:T(8,128)(2,1)S(1)} %copy-done.1, bf16[512,2048]{1,0:T(8,128)(2,1)S(1)} %copy-done, s32[1,2048]{1,0:T(1,128)S(1)} %bitcast.5), custom_call_target="tpu_custom_call" | custom-call | tf_op jit(solution)/shard_map/pallas_call | solution.py:391
  42.9 2.6 %fusion = bf16[1,512,2048]{2,1,0:T(8,128)(2,1)} fusion(bf16[512,512]{1,0:T(8,128)(2,1)S(1)} %get-tuple-element.7, bf16[512,2048]{1,0:T(8,128)(2,1)S(1)} %get-tuple-element.8), kind=kOutput, calls=%fused_computation.1 | convolution fusion | flops 1074790400 | bytes 4718592 | tf_op jit(solution)/shard_map/dot_general | solution.py:435
Async XLA Ops:
  1.3 1.6 %copy-start = (bf16[512,2048]{1,0:T(8,128)(2,1)S(1)}, bf16[512,2048]{1,0:T(8,128)(2,1)}, u32[]{:S(2)}) copy-start(bf16[512,2048]{1,0:T(8,128)(2,1)} %coeffs_in.1) | copy-start | bytes 6291460
  2.9 1.2 %copy-start.1 = (bf16[2,512,512]{2,1,0:T(8,128)(2,1)S(1)}, bf16[2,512,512]{2,1,0:T(8,128)(2,1)}, u32[]{:S(2)}) copy-start(bf16[2,512,512]{2,1,0:T(8,128)(2,1)} %pert_in.1) | copy-start | bytes 3145732
  4.1 0.7 %copy-start.2 = (s32[2048]{0:T(1024)S(1)}, s32[2048]{0:T(1024)}, u32[]{:S(2)}) copy-start(s32[2048]{0:T(1024)} %param.10) | copy-start | bytes 24580
  4.8 0.7 %copy-start.3 = (f32[64]{0:T(128)S(1)}, f32[64]{0:T(128)}, u32[]{:S(2)}) copy-start(f32[64]{0:T(128)} %amplitude.1) | copy-start | bytes 772

commit v3 on v2

--- a/solution.py
+++ b/solution.py
@@ -34,6 +34,7 @@
     coeffs_in,
     batch_in,
     reach_out,
+    release_out,
     release,
     pert,
     coeffs,
@@ -82,6 +83,7 @@
     ]
     for fetch in fetches:
         fetch.start()
+    store = pltpu.make_async_copy(release, release_out, in_sem.at[3])
     barrier = pltpu.get_barrier_semaphore()
     for mate in (core_mate, x_mate):
         pl.semaphore_signal(barrier, inc=1, device_id={"tm": mate}, device_id_type=MESH)
@@ -173,6 +175,7 @@
         for b in range(amplitude.shape[0]):
             column_scale = jnp.where(ids == b, amplitude[b], column_scale)
         release[...] = (coeffs[...].astype(jnp.float32) * column_scale).astype(jnp.bfloat16)
+        store.start()
 
     pl.when(has_prev)(make_release)
 
@@ -220,28 +223,61 @@
             def _():
                 chain(lane, s).start()
 
+    def split_quad():
+        high, low = halves(quad[...])
+        quad_high[...] = high
+        quad_low[...] = low
+
     @pl.when(has_prev)
     def _():
-        @pl.loop(0, per_core)
-        def _(j):
-            x_copy(1 - x, core, j).wait_recv()
-            x_forward(core, j).start()
+        high, low = halves(chip2[x])
+        right_high[...] = high
+        right_low[...] = low
+        per_group = per_core // QUAD
+
+        @pl.when(x == 0)
+        def _():
+            quad[...] = chip2[0]
+
+        def add_group(g):
+            for j in range(g * per_group, (g + 1) * per_group):
+                x_forward(1 - core, j).wait_recv()
+            rows = slice(g * group, (g + 1) * group)
+
+            @pl.when(x == 1)
+            def _():
+                quad[rows] = times(
+                    chip2[0, rows], chip2[1, rows], right_high[...], right_low[...]
+                )
+
+            @pl.when(x == 0)
+            def _():
+                high, low = halves(chip2[1, rows])
+                left_high, left_low = right_high[:, rows], right_low[:, rows]
+                quad[...] += mul(left_high, high) + (mul(left_high, low) + mul(left_low, high))
+                quad[rows] += chip2[1, rows]
+
+        for g in range(QUAD):
+
+            @pl.loop(g * per_group, (g + 1) * per_group)
+            def _(j):
+                x_copy(1 - x, core, j).wait_recv()
+                x_forward(core, j).start()
+
+            if g:
+                add_group(g - 1)
+        add_group(QUAD - 1)
+        split_quad()
 
     pl.when(first)(make_release)
 
-    @pl.when(gets_x)
+    @pl.when(jnp.logical_and(first, x == 1))
     def _():
         @pl.loop(0, per_core)
         def _(j):
             x_forward(1 - core, j).wait_recv()
 
-        high, low = halves(chip2[1])
-        right_high[...] = high
-        right_low[...] = low
         quad[...] = times(chip2[0], chip2[1], right_high[...], right_low[...])
-        high, low = halves(quad[...])
-        quad_high[...] = high
-        quad_low[...] = low
 
     def make_within():
         @pl.when(lane == 0)
@@ -341,6 +377,7 @@
 
         finish_half(1 - x)
 
+    store.wait()
     for g in range(QUAD):
         to_core(core, g).wait_send()
 
@@ -395,8 +432,9 @@
             jax.ShapeDtypeStruct((order, columns), bf16),
         ),
         in_specs=[smem, smem, smem, anywhere, anywhere, anywhere],
-        out_specs=(vmem, vmem),
+        out_specs=(vmem, anywhere),
         scratch_shapes=[
+            pltpu.VMEM((order, columns), bf16),
             pltpu.VMEM(perturbation.shape, bf16),
             pltpu.VMEM((order, columns), bf16),
             pltpu.VMEM((1, columns), jnp.int32),
@@ -411,7 +449,7 @@
             pltpu.VMEM(square, bf16),
             pltpu.VMEM(square, bf16),
             pltpu.VMEM(square, bf16),
-            pltpu.SemaphoreType.DMA((3,)),
+            pltpu.SemaphoreType.DMA((4,)),
             sems(QUAD),
             sems(UNITS // 2),
             sems(UNITS // 2),
@@ -422,7 +460,7 @@
             sems(UNITS // QUAD),
         ],
         compiler_params=pltpu.CompilerParams(
-            collective_id=0, has_side_effects=True, vmem_limit_bytes=48 * 1024 * 1024
+            collective_id=0, has_side_effects=True, vmem_limit_bytes=60 * 1024 * 1024
         ),
     )(
         hours_live,

time: 45.8 us -> 45.1 us (0.985)
  local copies, waits for them, and re-layouts: 4.16 us -> 0 us
  matrix products: 2.58 us -> 4.35 us
  Pallas kernels: 37.5 us -> 38.9 us
    unnamed x8 -> x0, local copies, waits for them, and re-layouts: 4.16 us -> none
    dot_general x1, matrix products: 2.58 us -> 4.35 us  [on_device(): panel = jnp.dot(reach, release, preferred_element_type=jnp.float32)]
    pallas_call x1, Pallas kernels: 37.5 us -> 38.9 us  [on_device(): pl.pallas_call(functools.partial(kernel, count), out_shape=(jax.ShapeDtyp...]
where the time goes in v3:
time: 45.1 us; the launch traced here: 44.6 us
  Pallas kernels  38.9 us (86%)
  matrix products  4.35 us (10%)
  between operations  1.3 us (3%)
    pallas_call x1, Pallas kernels, on_device(): pl.pallas_call(functools.partial(kernel, count), out_shape=(jax.ShapeDtyp...  38.9 us
    dot_general x1, matrix products, on_device(): panel = jnp.dot(reach, release, preferred_element_type=jnp.float32)  4.35 us

profile of v3, /device:TPU:25, one launch (start us, length us, event | category | flops | bytes accessed | tf_op | source)
XLA Modules:
  0.0 44.6 jit_solution(10762174466954597235)
XLA Ops:
  1.3 38.9 %shard_map.64 = (bf16[512,512]{1,0:T(8,128)(2,1)}, bf16[512,2048]{1,0:T(8,128)(2,1)}) custom-call(s32[1]{0:T(128)S(6)} %copy.7.hours_live, s32[1]{0:T(128)S(6)} %copy.8.start_hour, f32[64]{0:T(128)} %amplitude.1, bf16[2,512,512]{2,1,0:T(8,128)(2,1)} %pert_in.1, bf16[512,2048]{1,0:T(8,128)(2,1)} %coeffs_in.1, s32[1,2048]{1,0:T(1,128)} %bitcast.5), custom_call_target="tpu_custom_call" | custom-call | tf_op jit(solution)/shard_map/pallas_call | solution.py:428
  40.2 4.3 %fusion = bf16[1,512,2048]{2,1,0:T(8,128)(2,1)} fusion(bf16[512,512]{1,0:T(8,128)(2,1)} %get-tuple-element.7, bf16[512,2048]{1,0:T(8,128)(2,1)} %get-tuple-element.8), kind=kOutput, calls=%fused_computation.1 | convolution fusion | flops 1074790400 | bytes 4718592 | tf_op jit(solution)/shard_map/dot_general | solution.py:473

commit v4 on v3

--- a/solution.py
+++ b/solution.py
@@ -9,6 +9,7 @@
 MESH = pl.DeviceIdType.MESH
 QUAD = 4
 UNITS = 32
+LAG = 4
 
 
 def halves(value):
@@ -29,13 +30,13 @@
     count,
     hours_live,
     start_hour,
-    amplitude,
+    amplitude_in,
     pert_in,
     coeffs_in,
     batch_in,
     reach_out,
-    release_out,
     release,
+    amplitude,
     pert,
     coeffs,
     batch,
@@ -79,11 +80,17 @@
 
     fetches = [
         pltpu.make_async_copy(src, dst, in_sem.at[i])
-        for i, (src, dst) in enumerate(((pert_in, pert), (coeffs_in, coeffs), (batch_in, batch)))
+        for i, (src, dst) in enumerate(
+            (
+                (pert_in, pert),
+                (coeffs_in, coeffs),
+                (batch_in, batch),
+                (amplitude_in, amplitude),
+            )
+        )
     ]
     for fetch in fetches:
         fetch.start()
-    store = pltpu.make_async_copy(release, release_out, in_sem.at[3])
     barrier = pltpu.get_barrier_semaphore()
     for mate in (core_mate, x_mate):
         pl.semaphore_signal(barrier, inc=1, device_id={"tm": mate}, device_id_type=MESH)
@@ -168,14 +175,13 @@
                 x_copy(x, core, j).start()
 
     def make_release():
-        fetches[1].wait()
-        fetches[2].wait()
+        for fetch in fetches[1:]:
+            fetch.wait()
         ids = batch[...]
         column_scale = jnp.zeros(ids.shape, jnp.float32)
         for b in range(amplitude.shape[0]):
             column_scale = jnp.where(ids == b, amplitude[b], column_scale)
         release[...] = (coeffs[...].astype(jnp.float32) * column_scale).astype(jnp.bfloat16)
-        store.start()
 
     pl.when(has_prev)(make_release)
 
@@ -257,15 +263,17 @@
                 quad[...] += mul(left_high, high) + (mul(left_high, low) + mul(left_low, high))
                 quad[rows] += chip2[1, rows]
 
-        for g in range(QUAD):
-
-            @pl.loop(g * per_group, (g + 1) * per_group)
+        def pass_on(start, stop):
+            @pl.loop(start, stop)
             def _(j):
                 x_copy(1 - x, core, j).wait_recv()
                 x_forward(core, j).start()
 
-            if g:
-                add_group(g - 1)
+        ahead = per_group // 2
+        pass_on(0, per_group + ahead)
+        for g in range(QUAD - 1):
+            add_group(g)
+            pass_on((g + 1) * per_group + ahead, min((g + 2) * per_group + ahead, per_core))
         add_group(QUAD - 1)
         split_quad()
 
@@ -333,9 +341,9 @@
                 )
                 chain(lane, s).start()
 
-            @pl.when(s > 1)
+            @pl.when(s >= LAG)
             def _():
-                share_x(s - 2)
+                share_x(s - LAG)
 
     pl.when(has_next)(make_within)
 
@@ -362,8 +370,8 @@
 
     @pl.when(has_prev)
     def _():
-        share_x(per_lane - 2)
-        share_x(per_lane - 1)
+        for s in range(per_lane - LAG, per_lane):
+            share_x(s)
 
         @pl.loop(0, per_lane)
         def _(s):
@@ -377,7 +385,6 @@
 
         finish_half(1 - x)
 
-    store.wait()
     for g in range(QUAD):
         to_core(core, g).wait_send()
 
@@ -421,7 +428,7 @@
     columns = release_coeffs.shape[1]
     vmem = pl.BlockSpec(memory_space=pltpu.VMEM)
     smem = pl.BlockSpec(memory_space=pltpu.SMEM)
-    anywhere = pl.BlockSpec(memory_space=pl.ANY)
+    hbm = pl.BlockSpec(memory_space=pltpu.HBM)
     f32, bf16 = jnp.float32, jnp.bfloat16
     square = (order, order)
     sems = lambda n: pltpu.SemaphoreType.DMA((2, n))
@@ -431,10 +438,10 @@
             jax.ShapeDtypeStruct(square, bf16),
             jax.ShapeDtypeStruct((order, columns), bf16),
         ),
-        in_specs=[smem, smem, smem, anywhere, anywhere, anywhere],
-        out_specs=(vmem, anywhere),
+        in_specs=[smem, smem, hbm, hbm, hbm, hbm],
+        out_specs=(vmem, vmem),
         scratch_shapes=[
-            pltpu.VMEM((order, columns), bf16),
+            pltpu.SMEM(batch_amplitude.shape, f32),
             pltpu.VMEM(perturbation.shape, bf16),
             pltpu.VMEM((order, columns), bf16),
             pltpu.VMEM((1, columns), jnp.int32),
@@ -460,15 +467,15 @@
             sems(UNITS // QUAD),
         ],
         compiler_params=pltpu.CompilerParams(
-            collective_id=0, has_side_effects=True, vmem_limit_bytes=60 * 1024 * 1024
+            collective_id=0, has_side_effects=True, vmem_limit_bytes=40 * 1024 * 1024
         ),
     )(
         hours_live,
         start_hour,
-        batch_amplitude,
-        perturbation,
-        release_coeffs,
-        batch_of_column[None, :],
+        *(
+            pltpu.with_memory_space_constraint(value, pltpu.HBM)
+            for value in (batch_amplitude, perturbation, release_coeffs, batch_of_column[None, :])
+        ),
     )
     panel = jnp.dot(reach, release, preferred_element_type=jnp.float32)
     return panel.astype(bf16)[None, :, :]

time: 45.1 us -> 40.3 us (0.89)
  Pallas kernels: 38.9 us -> 36.3 us
  matrix products: 4.35 us -> 2.58 us
    pallas_call x1, Pallas kernels: 38.9 us -> 36.3 us  [on_device(): pl.pallas_call(functools.partial(kernel, count), out_shape=(jax.ShapeDtyp...]
    dot_general x1, matrix products: 4.35 us -> 2.58 us  [on_device(): panel = jnp.dot(reach, release, preferred_element_type=jnp.float32)]
where the time goes in v4:
time: 40.3 us; the launch traced here: 40.2 us
  Pallas kernels  36.3 us (90%)
  matrix products  2.58 us (6%)
  between operations  1.3 us (3%)
    pallas_call x1, Pallas kernels, on_device(): pl.pallas_call(functools.partial(kernel, count), out_shape=(jax.ShapeDtyp...  36.3 us
    dot_general x1, matrix products, on_device(): panel = jnp.dot(reach, release, preferred_element_type=jnp.float32)  2.58 us

profile of v4, /device:TPU:25, one launch (start us, length us, event | category | flops | bytes accessed | tf_op | source)
XLA Modules:
  0.0 40.2 jit_solution(7908772021172759700)
XLA Ops:
  1.3 36.3 %shard_map.64 = (bf16[512,512]{1,0:T(8,128)(2,1)S(1)}, bf16[512,2048]{1,0:T(8,128)(2,1)S(1)}) custom-call(s32[1]{0:T(128)S(6)} %copy.7.hours_live, s32[1]{0:T(128)S(6)} %copy.8.start_hour, f32[64]{0:T(128)} %amplitude_in.1, bf16[2,512,512]{2,1,0:T(8,128)(2,1)} %pert_in.1, bf16[512,2048]{1,0:T(8,128)(2,1)} %coeffs_in.1, s32[1,2048]{1,0:T(1,128)} %bitcast.5), custom_call_target="tpu_custom_call" | custom-call | tf_op jit(solution)/shard_map/pallas_call | solution.py:435
  37.6 2.6 %fusion = bf16[1,512,2048]{2,1,0:T(8,128)(2,1)} fusion(bf16[512,512]{1,0:T(8,128)(2,1)S(1)} %get-tuple-element.7, bf16[512,2048]{1,0:T(8,128)(2,1)S(1)} %get-tuple-element.8), kind=kOutput, calls=%fused_computation.1 | convolution fusion | flops 1074790400 | bytes 4718592 | tf_op jit(solution)/shard_map/dot_general | solution.py:480

commit v5 on v4

--- a/solution.py
+++ b/solution.py
@@ -23,7 +23,9 @@
 
 def times(left, right, right_high, right_low):
     high, low = halves(left)
-    return left + right + (mul(high, right_high) + (mul(high, right_low) + mul(low, right_high)))
+    rows = left.shape[0]
+    both = mul(jnp.concatenate([high, low], axis=0), right_high)
+    return left + right + (both[:rows] + (mul(high, right_low) + both[rows:]))
 
 
 def kernel(
@@ -330,8 +332,6 @@
         @pl.loop(0, per_lane)
         def _(s):
             chain(lane, s).wait_recv()
-            shared(ex_sem, lane, x_mate, s).start()
-            shared(ef_sem, lane, core_mate, s).start()
 
             @pl.when(has_next)
             def _():
@@ -341,6 +341,9 @@
                 )
                 chain(lane, s).start()
 
+            shared(ex_sem, lane, x_mate, s).start()
+            shared(ef_sem, lane, core_mate, s).start()
+
             @pl.when(s >= LAG)
             def _():
                 share_x(s - LAG)
@@ -368,9 +371,31 @@
             times(reach_in[rows], within[rows], right_high[...], right_low[...]), start, half
         )
 
+    def drain():
+        for g in range(QUAD):
+            to_core(core, g).wait_send()
+
+        @pl.when(sends_x)
+        def _():
+            @pl.loop(0, per_core)
+            def _(j):
+                x_copy(x, core, j).wait_send()
+
+        @pl.when(gets_x)
+        def _():
+            @pl.loop(0, per_core)
+            def _(j):
+                x_forward(core, j).wait_send()
+
+        @pl.when(jnp.logical_and(first, x == 1))
+        def _():
+            @pl.loop(0, per_lane)
+            def _(s):
+                send_back(s).wait_send()
+
     @pl.when(has_prev)
     def _():
-        for s in range(per_lane - LAG, per_lane):
+        for s in range(per_lane - LAG, per_lane - 2):
             share_x(s)
 
         @pl.loop(0, per_lane)
@@ -378,6 +403,9 @@
             shared(ef_sem, core_lane, core_mate, s).wait_recv()
 
         finish_half(x)
+        for s in range(per_lane - 2, per_lane):
+            share_x(s)
+        drain()
 
         @pl.loop(0, per_lane)
         def _(s):
@@ -385,26 +413,7 @@
 
         finish_half(1 - x)
 
-    for g in range(QUAD):
-        to_core(core, g).wait_send()
-
-    @pl.when(sends_x)
-    def _():
-        @pl.loop(0, per_core)
-        def _(j):
-            x_copy(x, core, j).wait_send()
-
-    @pl.when(gets_x)
-    def _():
-        @pl.loop(0, per_core)
-        def _(j):
-            x_forward(core, j).wait_send()
-
-    @pl.when(jnp.logical_and(first, x == 1))
-    def _():
-        @pl.loop(0, per_lane)
-        def _(s):
-            send_back(s).wait_send()
+    pl.when(first)(drain)
 
     @pl.when(has_next)
     def _():
@@ -419,6 +428,10 @@
             shared(ex_sem, lane, x_mate, s).wait_send()
             shared(ef_sem, lane, core_mate, s).wait_send()
             shared(exf_sem, x_lane, core_mate, s).wait_send()
+
+
+def panel_tile(reach, release, panel):
+    panel[0] = mul(reach[...], release[...]).astype(panel.dtype)
 
 
 def on_device(
@@ -477,8 +490,15 @@
             for value in (batch_amplitude, perturbation, release_coeffs, batch_of_column[None, :])
         ),
     )
-    panel = jnp.dot(reach, release, preferred_element_type=jnp.float32)
-    return panel.astype(bf16)[None, :, :]
+    width = 512
+    return pl.pallas_call(
+        panel_tile,
+        out_shape=jax.ShapeDtypeStruct((1, order, columns), bf16),
+        grid=(columns // width,),
+        in_specs=[vmem, pl.BlockSpec((order, width), lambda i: (0, i))],
+        out_specs=pl.BlockSpec((1, order, width), lambda i: (0, 0, i)),
+        compiler_params=pltpu.CompilerParams(vmem_limit_bytes=16 * 1024 * 1024),
+    )(reach, release)
 
 
 def solution(mesh):

time: 40.3 us -> 40.4 us (level)
  Pallas kernels: 36.3 us -> 39 us
  matrix products: 2.58 us -> 0 us
    pallas_call x0 -> x1, Pallas kernels: none -> 3.06 us  [on_device(): pl.pallas_call(panel_tile, out_shape=jax.ShapeDtypeStruct((1, order, colu...]
    dot_general x1 -> x0, matrix products: 2.58 us -> none  [on_device(): panel = jnp.dot(reach, release, preferred_element_type=jnp.float32)]
where the time goes in v5:
time: 40.4 us; the launch traced here: 40.3 us
  Pallas kernels  39 us (97%)
  between operations  1.3 us (3%)
    pallas_call x1, Pallas kernels, on_device(): pl.pallas_call(functools.partial(kernel, count), out_shape=(jax.ShapeDtyp...  35.9 us
    pallas_call x1, Pallas kernels, on_device(): pl.pallas_call(panel_tile, out_shape=jax.ShapeDtypeStruct((1, order, colu...  3.06 us

profile of v5, /device:TPU:25, one launch (start us, length us, event | category | flops | bytes accessed | tf_op | source)
XLA Modules:
  0.0 40.3 jit_solution(12160853521711137405)
XLA Ops:
  1.3 35.9 %shard_map.64 = (bf16[512,512]{1,0:T(8,128)(2,1)S(1)}, bf16[512,2048]{1,0:T(8,128)(2,1)S(1)}) custom-call(s32[1]{0:T(128)S(6)} %copy.7.hours_live, s32[1]{0:T(128)S(6)} %copy.8.start_hour, f32[64]{0:T(128)} %amplitude_in.1, bf16[2,512,512]{2,1,0:T(8,128)(2,1)} %pert_in.1, bf16[512,2048]{1,0:T(8,128)(2,1)} %coeffs_in.1, s32[1,2048]{1,0:T(1,128)} %bitcast.1), custom_call_target="tpu_custom_call" | custom-call | tf_op jit(solution)/shard_map/pallas_call | solution.py:448
  37.2 3.1 %shard_map.65 = bf16[1,512,2048]{2,1,0:T(8,128)(2,1)} custom-call(bf16[512,512]{1,0:T(8,128)(2,1)S(1)} %get-tuple-element.7.reach, bf16[512,2048]{1,0:T(8,128)(2,1)S(1)} %get-tuple-element.8.release), custom_call_target="tpu_custom_call" | custom-call | tf_op jit(solution)/shard_map/pallas_call | solution.py:494
